TPU v7x, 1024 devices: a whole 4x4x32 slice. The times are simulated.
1024 devices in a mesh: grp: 16 (over x, y), loc: 64 (over z, core).
Axes of the slice: x: 4, y: 4, z: 32, core: 2. Of those that a mesh axis runs over, the one named last changes fastest.
Arguments:
- tokens: bfloat16 [4096, 7168], P('loc', 'grp'), may hold values from -6 to 6
- expert_ids: int32 [4096, 8], P('loc'), may hold values from 0 to 63, all different within a row; in each aligned block of 64 rows (0 to 63, 64 to 127, ...) at most 16 rows name the same one
- route_weight: float32 [4096, 8], P('loc'), may hold values from 0.1 to 1
- w_gate: bfloat16 [64, 7168, 1024], P('loc', 'grp'), may hold values from -0.0625 to 0.0625
- w_up: bfloat16 [64, 7168, 1024], P('loc', 'grp'), may hold values from -0.0625 to 0.0625
- w_down: bfloat16 [64, 1024, 7168], P('loc', None, 'grp'), may hold values from -0.1875 to 0.1875
Outputs:
- mixed: bfloat16 [4096, 7168], P('loc', 'grp')
Inputs may be any that keep to these rules, and one draw needn't show every extreme that they name: `expert_ids`: each row names 8 different experts. Among the rows of one index of loc no expert is named more than 16 times, a bound that some block reaches.
All inputs are finite; a program needn't handle non-finite values.
Results may differ from a plain program's by a relative error of at most 0.03.
Values may be sent and summed in bfloat16 or wider, within the bound.
A program may use at most 32 MiB of HBM per device.

v0:
```python
import jax
import jax.numpy as jnp
from jax import lax
from jax.sharding import PartitionSpec as P


def shards(tokens, expert_ids, route_weight, w_gate, w_up, w_down):
    token_count, feature_part = tokens.shape
    route_count = expert_ids.shape[1]
    expert_count = lax.axis_size("loc")
    capacity = min(token_count, 2 * token_count * route_count // expert_count)
    flat_ids = expert_ids.reshape(-1)
    expert_hits = (flat_ids[:, None] == jnp.arange(expert_count, dtype=jnp.int32)[None, :]).astype(
        jnp.int32
    )
    position = jnp.sum(jnp.cumsum(expert_hits, axis=0) * expert_hits, axis=1) - 1
    target = flat_ids * capacity + position
    select = (
        target[:, None] == jnp.arange(expert_count * capacity, dtype=jnp.int32)[None, :]
    ).astype(jnp.bfloat16)
    placing = jnp.sum(select.reshape(token_count, route_count, expert_count * capacity), axis=1)
    outgoing = lax.dot_general(
        placing, tokens, (((0,), (0,)), ((), ())), preferred_element_type=jnp.float32
    )
    outgoing = outgoing.astype(jnp.bfloat16).reshape(expert_count, capacity, feature_part)
    arrived = lax.all_to_all(outgoing, "loc", split_axis=0, concat_axis=0, tiled=True).reshape(
        expert_count * capacity, feature_part
    )
    row_count = arrived.shape[0]
    gate_part = w_gate[0]
    up_part = w_up[0]
    down_part = w_down[0]
    gate_term = lax.dot_general(
        gate_part, arrived, (((0,), (1,)), ((), ())), preferred_element_type=jnp.float32
    )
    up_term = lax.dot_general(
        up_part, arrived, (((0,), (1,)), ((), ())), preferred_element_type=jnp.float32
    )
    summed = lax.psum_scatter(
        jnp.concatenate([gate_term, up_term], axis=1).astype(jnp.bfloat16),
        "grp",
        scatter_dimension=0,
        tiled=True,
    ).astype(jnp.float32)
    hidden = (jax.nn.silu(summed[:, :row_count]) * summed[:, row_count:]).astype(jnp.bfloat16)
    result = lax.dot_general(
        lax.all_gather(hidden, "grp", axis=0, tiled=True),
        down_part,
        (((0,), (0,)), ((), ())),
        preferred_element_type=jnp.float32,
    )
    expert_out = result.astype(jnp.bfloat16).reshape(expert_count, capacity, feature_part)
    returned = lax.all_to_all(expert_out, "loc", split_axis=0, concat_axis=0, tiled=True).reshape(
        expert_count * capacity, feature_part
    )
    picked = jnp.dot(select, returned, preferred_element_type=jnp.float32).reshape(
        token_count, route_count, feature_part
    )
    mixed = jnp.sum(picked * route_weight[:, :, None], axis=1)
    return mixed.astype(jnp.bfloat16)


def solution(mesh):
    in_specs = (
        P("loc", "grp"),
        P("loc", None),
        P("loc", None),
        P("loc", "grp", None),
        P("loc", "grp", None),
        P("loc", None, "grp"),
    )
    out_specs = P("loc", "grp")
    return jax.shard_map(shards, mesh=mesh, in_specs=in_specs, out_specs=out_specs, check_vma=False)
```

profile of v0, /device:TPU:2, one launch (start us, length us, event | category | flops | bytes accessed | tf_op | source)
XLA Modules:
  0.0 490.4 jit_solution(17618211640391526910)
XLA Ops:
  6.5 0.0 copy-start
  6.5 0.0 reduce-scatter.4.cloned.1.call-start
  6.5 0.9 copy.39
  7.4 0.1 eq.65
  7.5 0.1 eq.61
  7.6 1.2 reduce-window.6
  8.8 0.2 slice_reduce_fusion
  9.1 0.1 fusion.17
  9.2 0.1 sub.7
  9.3 0.1 copy.42
  9.4 0.7 multiply_add_fusion
  10.1 0.1 copy.43
  10.2 0.7 fusion.10
  10.8 1.3 convolution_convert_fusion.1
  12.1 0.5 copy.45
  12.7 139.8 %all_to_all.10 = bf16[64,16,448]{2,1,0:T(8,128)(2,1)S(1)} all-to-all(bf16[64,16,448]{2,1,0:T(8,128)(2,1)S(1)} %bitcast.48), channel_id=1, replica_groups=mesh['grp'=16,'loc'=64] {'loc'}, dimensions={0} | all-to-all | bytes 1835008 | tf_op jit(solution)/shard_map/all_to_all | solution.py:26
  152.5 0.0 copy-done
  152.5 0.0 copy-start.2
  152.5 1.3 convert_bitcast_fusion
  153.8 0.0 copy-done.2
  153.8 1.3 convert_bitcast_fusion.1
  155.1 2.4 pad_maximum_fusion
  157.5 6.5 %copy.52 = bf16[1024,2048]{1,0:T(8,128)(2,1)} copy(bf16[1024,2048]{0,1:T(8,128)(2,1)} %pad_maximum_fusion) | data formatting | bytes 8388608
  164.0 0.0 copy-start.3
  164.0 0.0 reduce-scatter.4.cloned.1.call-update
  164.0 0.0 all-gather.2.cloned.1.call-start
  164.0 94.5 %reduce-scatter.4.cloned.1.call-done = bf16[64,2048]{1,0:T(8,128)(2,1)} async-done(((bf16[1024,2048]{1,0:T(8,128)(2,1)}), bf16[64,2048]{1,0:T(8,128)(2,1)}) %reduce-scatter.4.cloned.1.call-update) | async-done | bytes 262160 | tf_op jit(solution)/shard_map/reduce_scatter | solution.py:39
  258.6 1.0 convert_element_type.30
  259.6 0.7 fusion.15
  260.3 0.0 all-gather.2.cloned.1.call-update
  260.3 83.4 %all-gather.2.cloned.1.call-done = bf16[1024,1024]{1,0:T(8,128)(2,1)} async-done(((bf16[64,1024]{1,0:T(8,128)(2,1)}), bf16[1024,1024]{1,0:T(8,128)(2,1)}) %all-gather.2.cloned.1.call-update) | async-done | bytes 2097168 | tf_op jit(solution)/shard_map/all_gather | solution.py:47
  343.7 0.0 copy-done.3
  343.7 2.7 convolution_convert_fusion
  346.5 0.0 copy-start.1
  346.5 1.3 copy.47
  347.8 23.5 %all-to-all-start.1 = ((bf16[64,16,448]{2,1,0:T(8,128)(2,1)}), bf16[64,16,448]{2,1,0:T(8,128)(2,1)S(1)}, u32[]{:S(2)}, u32[]{:S(2)}) async-start(bf16[64,16,448]{2,1,0:T(8,128)(2,1)} %bitcast.9), calls=%async_computation.1 | async-start | bytes 2097152 | tf_op jit(solution)/shard_map/all_to_all | solution.py:53
  371.3 0.0 copy-done.1
  371.3 0.1 copy.49
  371.4 110.6 %all-to-all-done.1 = bf16[64,16,448]{2,1,0:T(8,128)(2,1)S(1)} async-done(((bf16[64,16,448]{2,1,0:T(8,128)(2,1)}), bf16[64,16,448]{2,1,0:T(8,128)(2,1)S(1)}, u32[]{:S(2)}, u32[]{:S(2)}) %all-to-all-start.1) | async-done | bytes 917536 | tf_op jit(solution)/shard_map/all_to_all | solution.py:53
  482.0 1.6 fusion.7
  (4 shorter events, 0.1 us)
Async XLA Ops:
  6.5 146.0 %copy-start = (bf16[1,448,1024]{2,1,0:T(8,128)(2,1)S(1)}, bf16[1,448,1024]{2,1,0:T(8,128)(2,1)}, u32[]{:S(2)}) copy-start(bf16[1,448,1024]{2,1,0:T(8,128)(2,1)} %param.10) | copy-start | bytes 2752516
  6.5 252.0 %reduce-scatter.4.cloned.1.call-start = ((), (), s32[]{:S(2)}) async-start(), calls=%async_computation.4 | async-start | bytes 4456448 | tf_op jit(solution)/shard_map/reduce_scatter | solution.py:39
  152.5 1.3 copy-start.2
  164.0 179.8 %copy-start.3 = (bf16[1,1024,448]{1,2,0:T(8,128)(2,1)S(1)}, bf16[1,1024,448]{1,2,0:T(8,128)(2,1)}, u32[]{:S(2)}) copy-start(bf16[1,1024,448]{1,2,0:T(8,128)(2,1)} %param.11) | copy-start | bytes 2752516
  164.0 179.7 %all-gather.2.cloned.1.call-start = ((), (), s32[]{:S(2)}) async-start(), calls=%async_computation.3 | async-start | bytes 2228224 | tf_op jit(solution)/shard_map/all_gather | solution.py:47
  346.5 24.9 %copy-start.1 = (f32[64,8]{0,1:T(8,128)S(1)}, f32[64,8]{0,1:T(8,128)}, u32[]{:S(2)}) copy-start(f32[64,8]{0,1:T(8,128)} %param.8) | copy-start | bytes 6148
  347.8 134.2 %all-to-all-start.1 = ((bf16[64,16,448]{2,1,0:T(8,128)(2,1)}), bf16[64,16,448]{2,1,0:T(8,128)(2,1)S(1)}, u32[]{:S(2)}, u32[]{:S(2)}) async-start(bf16[64,16,448]{2,1,0:T(8,128)(2,1)} %bitcast.9), calls=%async_computation.1 | async-start | bytes 2097152 | tf_op jit(solution)/shard_map/all_to_all | solution.py:53
Sparse Core Ops, SparseCore 0:
  164.1 94.4 reduce-scatter.3
  263.5 80.2 all-gather.1
where the time goes:
time: 491 us; the launch traced here: 490 us
  waiting for transfers between devices  289 us (59%)
  blocking collectives  140 us (29%)
  starting transfers between devices  23.6 us (5%)
  between operations  13.5 us (3%)
  local copies, waits for them, and re-layouts  9.95 us (2%)
  matrix products  8.09 us (2%)
  other arithmetic  6.89 us (1%)
    all_to_all x1, blocking collectives, shards(): lax.all_to_all(outgoing, 'loc', split_axis=0, concat_axis=0, tiled=True)  140 us
    all_to_all x1, waiting for transfers between devices, shards(): lax.all_to_all(expert_out, 'loc', split_axis=0, concat_axis=0, tiled=True)  111 us
    reduce_scatter x1, waiting for transfers between devices, shards(): lax.psum_scatter(jnp.concatenate([gate_term, up_term], axis=1).astype(jnp...  94.5 us
    all_gather x1, waiting for transfers between devices, shards(): lax.all_gather(hidden, 'grp', axis=0, tiled=True)  83.4 us
    all_to_all x1, starting transfers between devices, shards(): lax.all_to_all(expert_out, 'loc', split_axis=0, concat_axis=0, tiled=True)  23.5 us
  transfers between devices with their start and end apart: 3, of which 3 were waited for; matrix products, arithmetic and copies ran while one was open for 0% of the time, Pallas kernels for 0%

commit v1 on v0

v1 whole, which is shorter than its diff:
```python
import functools

import jax
import jax.numpy as jnp
from jax import lax
from jax.experimental import pallas as pl
from jax.experimental.pallas import tpu as pltpu
from jax.sharding import PartitionSpec as P

MESH = pl.DeviceIdType.MESH
BF16 = jnp.bfloat16
F32 = jnp.float32
SIDE = 4
META = 64


def remote(src, dst, send_sem, recv_sem, device):
    return pltpu.make_async_remote_copy(
        src_ref=src,
        dst_ref=dst,
        send_sem=send_sem,
        recv_sem=recv_sem,
        device_id=device,
        device_id_type=MESH,
    )


class RingSum:
    def __init__(self, source, place, right, left, recv, send, send_sem, recv_sem):
        self.source, self.place, self.right, self.left = source, place, right, left
        self.recv, self.send, self.send_sem, self.recv_sem = recv, send, send_sem, recv_sem

    def copy(self, c, kind):
        after, before = lax.rem(self.place + 1, SIDE), lax.rem(self.place + 3, SIDE)
        across = lax.rem(self.place + 2, SIDE)
        src = (
            lambda: self.source(c, 0, across),
            lambda: self.source(c, 1, after),
            lambda: self.source(c, 1, across),
            lambda: self.source(c, 0, before),
            lambda: self.send.at[c, 0],
            lambda: self.send.at[c, 1],
        )[kind]()
        to = (self.right, self.right, self.left, self.left, self.right, self.left)[kind]
        return remote(
            src, self.recv.at[c, kind], self.send_sem.at[c, kind], self.recv_sem.at[c, kind], to
        )

    def first(self, c):
        for kind in range(4):
            self.copy(c, kind).start()

    def second(self, c):
        after, before = lax.rem(self.place + 1, SIDE), lax.rem(self.place + 3, SIDE)
        self.copy(c, 0).wait_recv()
        total = self.source(c, 0, after)[...].astype(F32) + self.recv[c, 0].astype(F32)
        self.send[c, 0] = total.astype(BF16)
        self.copy(c, 4).start()
        self.copy(c, 2).wait_recv()
        total = self.source(c, 1, before)[...].astype(F32) + self.recv[c, 2].astype(F32)
        self.send[c, 1] = total.astype(BF16)
        self.copy(c, 5).start()

    def last(self, c):
        for kind in (1, 3, 4, 5):
            self.copy(c, kind).wait_recv()
        gate = self.source(c, 0, self.place)[...].astype(F32) + self.recv[c, 3].astype(F32)
        gate = gate + self.recv[c, 4].astype(F32)
        up = self.source(c, 1, self.place)[...].astype(F32) + self.recv[c, 1].astype(F32)
        up = up + self.recv[c, 5].astype(F32)
        return gate, up

    def finish(self, c):
        for kind in range(6):
            self.copy(c, kind).wait_send()


class RingGather:
    def __init__(self, piece, half, place, right, left, send_sem, recv_sem):
        self.piece, self.half, self.place, self.right, self.left = piece, half, place, right, left
        self.send_sem, self.recv_sem = send_sem, recv_sem

    def copy(self, c, kind, receiving=False):
        if receiving:
            at = lax.rem(self.place + (3, 1, 2, 2)[kind], SIDE)
        else:
            at = lax.rem(self.place + (0, 0, 3, 1)[kind], SIDE)
        ref = self.piece(c, at) if kind < 2 else self.half(c, at, kind - 2)
        to = (self.right, self.left, self.right, self.left)[kind]
        return remote(ref, ref, self.send_sem.at[c, kind], self.recv_sem.at[c, kind], to)

    def first(self, c):
        self.copy(c, 0).start()
        self.copy(c, 1).start()

    def second(self, c):
        self.copy(c, 0, True).wait_recv()
        self.copy(c, 2).start()
        self.copy(c, 1, True).wait_recv()
        self.copy(c, 3).start()

    def last(self, c):
        self.copy(c, 2, True).wait_recv()
        self.copy(c, 3, True).wait_recv()

    def finish(self, c):
        for kind in range(4):
            self.copy(c, kind).wait_send()


def kernel(
    steps, chunks, blk, wg_hbm, wu_hbm, wd_hbm, out_ref,
    tr, tl, wm, xb, xs, wg, wu, wd, pa, pb,
    ra1, sa1, rb1, sb1, qa, qb, ra2, sa2, rb2, sb2, ha, hb,
    ob, os_, or_, zr, szr, zl, szl,
    w_sem, tr_s, tr_r, tl_s, tl_r, x_s, x_r, o_s, o_r,
    a1_s, a1_r, b1_s, b1_r, a2_s, a2_r, b2_s, b2_r,
    ga1_s, ga1_r, gb1_s, gb1_r, ga2_s, ga2_r, gb2_s, gb2_r,
    zr_s, zr_r, zl_s, zl_r,
):
    features = wd.shape[1]
    grp, loc = lax.axis_index("grp"), lax.axis_index("loc")
    depth = lax.axis_size("loc") // 2
    x, y = grp // SIDE, lax.rem(grp, SIDE)
    z, core = loc // 2, lax.rem(loc, 2)
    x_right = (lax.rem(x + 1, SIDE) * SIDE + y, loc)
    x_left = (lax.rem(x + 3, SIDE) * SIDE + y, loc)
    y_right = (x * SIDE + lax.rem(y + 1, SIDE), loc)
    y_left = (x * SIDE + lax.rem(y + 3, SIDE), loc)
    z_right = (grp, lax.rem(z + 1, depth) * 2 + core)
    z_left = (grp, lax.rem(z + depth - 1, depth) * 2 + core)
    sibling = (grp, z * 2 + 1 - core)

    weight_copies = [
        pltpu.make_async_copy(wg_hbm.at[0], wg.at[pl.ds(META, features)], w_sem.at[0]),
        pltpu.make_async_copy(wu_hbm.at[0], wu.at[pl.ds(META, features)], w_sem.at[1]),
        pltpu.make_async_copy(wd_hbm.at[0], wd, w_sem.at[2]),
    ]
    for copy in weight_copies:
        copy.start()
    barrier = pltpu.get_barrier_semaphore()
    neighbours = (x_right, x_left, y_right, y_left, z_right, z_left, sibling)
    for device in neighbours:
        pl.semaphore_signal(barrier, inc=1, device_id=device, device_id_type=MESH)
    tl[0] = blk[...]
    wg[:META, :] = jnp.zeros((META, wg.shape[1]), BF16)
    wu[:META, :] = jnp.zeros((META, wu.shape[1]), BF16)
    pl.semaphore_wait(barrier, len(neighbours))

    def from_left(a):
        return lambda src: remote(src, tr.at[a], tr_s.at[a], tr_r.at[a], z_right)

    def from_right(a):
        return lambda src: remote(src, tl.at[a], tl_s.at[a], tl_r.at[a], z_left)

    from_left(0)(tl.at[0]).start()

    slots = wm.shape[2]
    block = wm.shape[3]
    row = lax.broadcasted_iota(jnp.int32, (slots, block), 0)
    mine = row < slots // 2
    slot = jnp.where(mine, row, row - slots // 2).astype(F32)
    earlier = (
        lax.broadcasted_iota(jnp.int32, (block, block), 0)
        < lax.broadcasted_iota(jnp.int32, (block, block), 1)
    ).astype(F32).astype(BF16)
    expert = loc.astype(F32)
    other = (z * 2 + 1 - core).astype(F32)

    def place(ref, a):
        meta = ref[a, :16, :META].astype(F32)
        ids, weights = meta[:8], meta[8:]
        hit, hit_other = ids == expert, ids == other
        count = lambda v: jnp.sum(v, axis=0, keepdims=True)
        hits = jnp.where(
            mine, count(jnp.where(hit, 1.0, 0.0)), count(jnp.where(hit_other, 1.0, 0.0))
        )
        scale = jnp.where(
            mine, count(jnp.where(hit, weights, 0.0)), count(jnp.where(hit_other, weights, 0.0))
        )
        position = jnp.dot(hits.astype(BF16), earlier, preferred_element_type=F32)
        chosen = jnp.where(position == slot, hits, 0.0)
        rows = jnp.dot(chosen.astype(BF16), ref[a], preferred_element_type=F32).astype(BF16)
        return rows, (chosen * scale).astype(BF16)

    def gather_step(c, j):
        a = c * 2 + j

        @pl.when(a > 0)
        def _():
            from_right(a)(tl.at[0]).wait_recv()

        @pl.when(a < steps - 1)
        def _():
            from_right(a + 1)(tl.at[a]).start()

        from_left(a)(tl.at[0]).wait_recv()

        @pl.when(a < steps - 1)
        def _():
            from_left(a + 1)(tr.at[a]).start()

        half = slots // 2
        for i, ref in enumerate((tr, tl)):
            rows, weights = place(ref, a)
            wm[a, i] = weights
            at = pl.ds(j * slots + i * half, half)
            xb[c, 0, at, :] = rows[:half]
            xs[c, at, :] = rows[half:]

    def x_copy(c):
        return remote(xs.at[c], xb.at[c, 1], x_s.at[c], x_r.at[c], sibling)

    def o_copy(c):
        at = pl.ds(c * 2, 2)
        return remote(os_.at[at], or_.at[at], o_s.at[c], o_r.at[c], sibling)

    sum_a1 = RingSum(
        lambda c, k, i: pa.at[c, k, i], x, x_right, x_left, ra1, sa1, a1_s, a1_r)
    sum_b1 = RingSum(
        lambda c, k, i: pb.at[c, k, i], y, y_right, y_left, rb1, sb1, b1_s, b1_r)
    sum_a2 = RingSum(
        lambda c, k, i: qa.at[c, k, i], y, y_right, y_left, ra2, sa2, a2_s, a2_r)
    sum_b2 = RingSum(
        lambda c, k, i: qb.at[c, k, i], x, x_right, x_left, rb2, sb2, b2_s, b2_r)
    rows_half = lambda ref, c, u, v, h: ref.at[c, u, v, pl.ds(h * 16, 16)]
    gather_a1 = RingGather(
        lambda c, i: ha.at[c, x, i], lambda c, i, h: rows_half(ha, c, x, i, h),
        y, y_right, y_left, ga1_s, ga1_r)
    gather_b1 = RingGather(
        lambda c, i: hb.at[c, y, i], lambda c, i, h: rows_half(hb, c, y, i, h),
        x, x_right, x_left, gb1_s, gb1_r)
    gather_a2 = RingGather(
        lambda c, i: ha.at[c, i], lambda c, i, h: ha.at[c, i, pl.ds(h * 2, 2)],
        x, x_right, x_left, ga2_s, ga2_r)
    gather_b2 = RingGather(
        lambda c, i: hb.at[c, i], lambda c, i, h: hb.at[c, i, pl.ds(h * 2, 2)],
        y, y_right, y_left, gb2_s, gb2_r)

    piece = pa.shape[4]

    def expand(c):
        x_copy(c).wait_recv()
        held = jnp.concatenate([xb[c, 0], xb[c, 1]], axis=0)
        for n in range(SIDE):
            for k, weight in enumerate((wg, wu)):
                part = jnp.dot(
                    held, weight[:, n * 256:(n + 1) * 256], preferred_element_type=F32
                ).astype(BF16)
                for i in range(SIDE):
                    low, lane = (i % 2) * piece, (i // 2) * 128
                    pa[c, k, n, i] = part[low:low + piece, lane:lane + 128]
                    pb[c, k, i, n] = part[2 * piece + low:3 * piece + low, lane:lane + 128]
        sum_a1.first(c)
        sum_b1.first(c)

    def stage2(c):
        sum_a1.second(c)
        sum_b1.second(c)

    def stage3(c):
        for ring, to, then in ((sum_a1, qa, sum_a2), (sum_b1, qb, sum_b2)):
            gate, up = ring.last(c)
            to[c, 0] = gate.astype(BF16)
            to[c, 1] = up.astype(BF16)
            then.first(c)

    def stage4(c):
        sum_a2.second(c)
        sum_b2.second(c)

    def stage5(c):
        gate, up = sum_a2.last(c)
        ha[c, x, y] = (gate / (1.0 + jnp.exp(-gate)) * up).astype(BF16)
        gather_a1.first(c)
        gate, up = sum_b2.last(c)
        hb[c, y, x] = (gate / (1.0 + jnp.exp(-gate)) * up).astype(BF16)
        gather_b1.first(c)

    def stage6(c):
        gather_a1.second(c)
        gather_b1.second(c)

    def stage7(c):
        gather_a1.last(c)
        gather_a2.first(c)
        gather_b1.last(c)
        gather_b2.first(c)

    def stage8(c):
        gather_a2.second(c)
        gather_b2.second(c)

    def contract(c):
        gather_a2.last(c)
        gather_b2.last(c)
        lines = [
            jnp.concatenate([ha[c, u, 2 * v + low] for u in range(SIDE) for v in range(2)], axis=1)
            for low in range(2)
        ] + [
            jnp.concatenate([hb[c, 2 * v + low, u] for u in range(SIDE) for v in range(2)], axis=1)
            for low in range(2)
        ]
        result = jnp.dot(
            jnp.concatenate(lines, axis=0), wd[...], preferred_element_type=F32
        ).astype(BF16)
        for j in range(2):
            for i in range(2):
                low = j * 32 + i * 16
                ob[c * 2 + j, i, :, :features] = result[low:low + 16]
                os_[c * 2 + j, i, :, :features] = result[64 + low:64 + low + 16]
        o_copy(c).start()

    def when(lag, t, stage):
        c = t - lag

        @pl.when(jnp.logical_and(c >= 0, c < chunks))
        def _():
            stage(c)

    def gather_first(c):
        gather_step(c, 0)

    def gather_second(c):
        gather_step(c, 1)
        x_copy(c).start()

    def turn(t, carry):
        when(0, t, gather_first)
        when(2, t, stage2)
        when(3, t, stage3)
        when(4, t, stage4)
        when(5, t, stage5)
        when(0, t, gather_second)

        @pl.when(t == 1)
        def _():
            for copy in weight_copies:
                copy.wait()

        when(1, t, expand)
        when(6, t, stage6)
        when(7, t, stage7)
        when(8, t, stage8)
        when(9, t, contract)
        when(10, t, lambda c: o_copy(c).wait_recv())
        return carry

    lax.fori_loop(0, chunks + 11, turn, 0)

    part = block // 2

    def to_left(a, h):
        return remote(szl.at[a, h], zl.at[a, h], zl_s.at[a, h], zl_r.at[a, h], z_left)

    def to_right(a, h):
        return remote(szr.at[a, h], zr.at[a, h], zr_s.at[a, h], zr_r.at[a, h], z_right)

    def share(a, i):
        held = jnp.concatenate([ob[a, i, :, :features], or_[a, i, :, :features]], axis=0)
        return lax.dot_general(
            wm[a, i], held, (((0,), (0,)), ((), ())), preferred_element_type=F32
        )

    def back(s, carry):
        a = steps - 1 - s
        left_share, right_share = share(a, 0), share(a, 1)
        for h in range(2):
            szl[a, h, :, :features] = left_share[h * part:(h + 1) * part].astype(BF16)

            @pl.when(a < steps - 1)
            def _():
                to_left(a + 1, h).wait_recv()
                szl[a, h, :, :features] = (
                    left_share[h * part:(h + 1) * part] + zl[a + 1, h, :, :features].astype(F32)
                ).astype(BF16)

            to_left(a, h).start()

            @pl.when(a > 0)
            def _():
                szr[a - 1, h, :, :features] = right_share[h * part:(h + 1) * part].astype(BF16)

                @pl.when(a < steps - 1)
                def _():
                    to_right(a, h).wait_recv()
                    szr[a - 1, h, :, :features] = (
                        right_share[h * part:(h + 1) * part] + zr[a, h, :, :features].astype(F32)
                    ).astype(BF16)

                to_right(a - 1, h).start()

        return carry

    lax.fori_loop(0, steps, back, 0)
    own = share(0, 1)
    for h in range(2):
        to_left(0, h).wait_recv()
        to_right(0, h).wait_recv()
        out_ref[h * part:(h + 1) * part, :] = (
            own[h * part:(h + 1) * part]
            + zl[0, h, :, :features].astype(F32)
            + zr[0, h, :, :features].astype(F32)
        ).astype(BF16)

    def finish(c, carry):
        x_copy(c).wait_send()
        o_copy(c).wait_send()
        for ring in (
            sum_a1, sum_b1, sum_a2, sum_b2, gather_a1, gather_b1, gather_a2, gather_b2,
        ):
            ring.finish(c)
        return carry

    lax.fori_loop(0, chunks, finish, 0)

    def finish_z(a, carry):
        from_left(a)(tl.at[0]).wait_send()
        for h in range(2):
            to_left(a, h).wait_send()

        @pl.when(a < steps - 1)
        def _():
            from_right(a + 1)(tl.at[0]).wait_send()
            for h in range(2):
                to_right(a, h).wait_send()

        return carry

    lax.fori_loop(0, steps, finish_z, 0)


def shards(tokens, expert_ids, route_weight, w_gate, w_up, w_down):
    block, features = tokens.shape
    top = expert_ids.shape[1]
    depth = lax.axis_size("loc") // 2
    steps = depth // 2
    chunks = steps // 2
    units = w_gate.shape[2]
    wide = features + META
    meta = jnp.concatenate([expert_ids.astype(BF16).T, route_weight.astype(BF16).T], axis=0)
    meta = jnp.pad(meta, ((0, block - 2 * top), (0, META - block)))
    blk = jnp.concatenate([meta, tokens], axis=1)
    piece = 32
    sem = lambda *shape: pltpu.SemaphoreType.DMA(shape)
    vmem = lambda *shape: pltpu.VMEM(shape, BF16)
    ring = (SIDE, piece, 128)
    scratch = [
        vmem(steps, block, wide), vmem(steps, block, wide),
        vmem(steps, 2, 32, block),
        vmem(chunks, 2, 64, wide), vmem(chunks, 64, wide),
        vmem(wide, units), vmem(wide, units), vmem(units, features),
        vmem(chunks, 2, SIDE, *ring), vmem(chunks, 2, SIDE, *ring),
        vmem(chunks, 6, *ring), vmem(chunks, 2, *ring),
        vmem(chunks, 6, *ring), vmem(chunks, 2, *ring),
        vmem(chunks, 2, *ring), vmem(chunks, 2, *ring),
        vmem(chunks, 6, piece, 128), vmem(chunks, 2, piece, 128),
        vmem(chunks, 6, piece, 128), vmem(chunks, 2, piece, 128),
        vmem(chunks, SIDE, *ring), vmem(chunks, SIDE, *ring),
        vmem(steps, 2, 16, wide), vmem(steps, 2, 16, wide), vmem(steps, 2, 16, wide),
        vmem(steps, 2, block // 2, wide), vmem(steps, 2, block // 2, wide),
        vmem(steps, 2, block // 2, wide), vmem(steps, 2, block // 2, wide),
        sem(3), sem(steps), sem(steps), sem(steps), sem(steps),
        sem(chunks), sem(chunks), sem(chunks), sem(chunks),
    ] + [sem(chunks, 6)] * 8 + [sem(chunks, 4)] * 8 + [sem(steps, 2)] * 4
    rows = chunks * 128
    return pl.pallas_call(
        functools.partial(kernel, steps, chunks),
        out_shape=jax.ShapeDtypeStruct((block, features), BF16),
        in_specs=[pl.BlockSpec(memory_space=pltpu.VMEM)]
        + [pl.BlockSpec(memory_space=pl.ANY)] * 3,
        out_specs=pl.BlockSpec(memory_space=pltpu.VMEM),
        scratch_shapes=scratch,
        compiler_params=pltpu.CompilerParams(
            collective_id=0, has_side_effects=True, vmem_limit_bytes=48 * 1024 * 1024
        ),
        cost_estimate=pl.CostEstimate(
            flops=6 * rows * features * units,
            bytes_accessed=6 * features * units,
            transcendentals=0,
        ),
    )(blk, w_gate, w_up, w_down)


def solution(mesh):
    in_specs = (
        P("loc", "grp"),
        P("loc", None),
        P("loc", None),
        P("loc", "grp", None),
        P("loc", "grp", None),
        P("loc", None, "grp"),
    )
    out_specs = P("loc", "grp")
    return jax.shard_map(shards, mesh=mesh, in_specs=in_specs, out_specs=out_specs, check_vma=False)
```

time: 491 us -> 175 us (0.36)
  waiting for transfers between devices: 289 us -> 0 us
  Pallas kernels: 0 us -> 171 us
  blocking collectives: 140 us -> 0 us
  starting transfers between devices: 23.6 us -> 0 us
  between operations: 13.5 us -> 0.05 us
  matrix products: 8.09 us -> 0 us
  local copies, waits for them, and re-layouts: 9.95 us -> 2.34 us
  other arithmetic: 6.89 us -> 1.64 us
    pallas_call x0 -> x1, Pallas kernels: none -> 171 us  [shards(): pl.pallas_call(functools.partial(kernel, steps, chunks), out_shape=jax.Sh...]
    all_to_all x1 -> x0, blocking collectives: 140 us -> none  [shards(): lax.all_to_all(outgoing, 'loc', split_axis=0, concat_axis=0, tiled=True)]
    all_to_all x1 -> x0, waiting for transfers between devices: 111 us -> none  [shards(): lax.all_to_all(expert_out, 'loc', split_axis=0, concat_axis=0, tiled=True)]
    reduce_scatter x1 -> x0, waiting for transfers between devices: 94.5 us -> none  [shards(): lax.psum_scatter(jnp.concatenate([gate_term, up_term], axis=1).astype(jnp...]
    all_gather x1 -> x0, waiting for transfers between devices: 83.4 us -> none  [shards(): lax.all_gather(hidden, 'grp', axis=0, tiled=True)]
    all_to_all x1 -> x0, starting transfers between devices: 23.5 us -> none  [shards(): lax.all_to_all(expert_out, 'loc', split_axis=0, concat_axis=0, tiled=True)]
    dot_general x5 -> x0, matrix products: 8.09 us -> none  [the longest x1 2.72 us: shards(): lax.dot_general(lax.all_gather(hidden, 'grp', axis=0, tiled=True), down_p...]
    unnamed x11 -> x8, local copies, waits for them, and re-layouts: 7.45 us -> 2.34 us
  transfers between devices with their start and end apart: 3 -> 0, of which waited for: 3 -> 0; matrix products, arithmetic and copies ran while one was open for 0% -> 0% of each run, Pallas kernels for 0% -> 0%
where the time goes in v1:
time: 175 us
  Pallas kernels  171 us (98%)
  local copies, waits for them, and re-layouts  2.34 us (1%)
    pallas_call x1, Pallas kernels, shards(): pl.pallas_call(functools.partial(kernel, steps, chunks), out_shape=jax.Sh...  171 us

profile of v1, /device:TPU:2, one launch (start us, length us, event | category | flops | bytes accessed | tf_op | source)
XLA Modules:
  0.0 175.1 jit_solution(10527620842305320191)
XLA Ops:
  0.0 0.0 copy-start.2
  0.0 0.7 convert_bitcast_fusion.1
  0.7 0.0 copy-done.2
  0.7 0.9 pad_maximum_fusion.blk
  1.7 0.0 copy-start
  1.7 0.0 copy-start.1
  1.7 1.6 copy.7.wd_hbm
  3.3 0.0 copy-done
  3.3 0.1 copy-done.1
  3.4 171.1 %shard_map.64 = bf16[64,448]{1,0:T(8,128)(2,1)S(1)} custom-call(bf16[64,512]{1,0:T(8,128)(2,1)S(1)} %pad_maximum_fusion.blk, bf16[1,448,1024]{2,1,0:T(8,128)(2,1)S(1)} %copy-done, bf16[1,448,1024]{2,1,0:T(8,128)(2,1)S(1)} %copy-done.1, bf16[1,1024,448]{2,1,0:T(8,128)(2,1)S(1)} %copy.7.wd_hbm), custom_call_target="tpu_custom_call" | custom-call | flops 2818572288 | bytes 2752512 | tf_op jit(solution)/shard_map/pallas_call | solution.py:467
  174.5 0.6 copy.9
  (2 shorter events, 0.0 us)
Async XLA Ops:
  0.0 0.7 copy-start.2
  1.7 1.6 copy-start
  1.7 1.7 copy-start.1

commit v2 on v0

v2 whole, which is shorter than its diff:
```python
import functools

import jax
import jax.numpy as jnp
from jax import lax
from jax.experimental import pallas as pl
from jax.experimental.pallas import tpu as pltpu
from jax.sharding import PartitionSpec as P

MESH = pl.DeviceIdType.MESH
BF16 = jnp.bfloat16
F32 = jnp.float32
SIDE = 4
PEERS = (2, 1, 3)
SUBS = 4
META = 64


def remote(src, dst, send_sem, recv_sem, device):
    return pltpu.make_async_remote_copy(
        src_ref=src,
        dst_ref=dst,
        send_sem=send_sem,
        recv_sem=recv_sem,
        device_id=device,
        device_id_type=MESH,
    )


class Scatter:
    def __init__(self, source, place, peers, recv, send_sem, recv_sem):
        self.source, self.place, self.peers, self.recv = source, place, peers, recv
        self.send_sem, self.recv_sem = send_sem, recv_sem

    def copy(self, c, d):
        return remote(
            self.source.at[c, lax.rem(self.place + d, SIDE)], self.recv.at[c, d - 1],
            self.send_sem.at[c, d - 1], self.recv_sem.at[c, d - 1], self.peers[d],
        )

    def start(self, c):
        for d in PEERS:
            self.copy(c, d).start()

    def total(self, c):
        for d in PEERS:
            self.copy(c, d).wait_recv()
        total = self.source[c, self.place].astype(F32)
        for d in PEERS:
            total = total + self.recv[c, d - 1].astype(F32)
        return total

    def finish(self, c):
        for d in PEERS:
            self.copy(c, d).wait_send()


class Gather:
    def __init__(self, piece, place, peers, send_sem, recv_sem):
        self.piece, self.place, self.peers = piece, place, peers
        self.send_sem, self.recv_sem = send_sem, recv_sem

    def copy(self, c, d, back=0):
        ref = self.piece(c, lax.rem(self.place + back, SIDE))
        return remote(
            ref, ref, self.send_sem.at[c, d - 1], self.recv_sem.at[c, d - 1], self.peers[d]
        )

    def start(self, c):
        for d in PEERS:
            self.copy(c, d).start()

    def wait(self, c):
        for d in PEERS:
            self.copy(c, d, SIDE - d).wait_recv()

    def finish(self, c):
        for d in PEERS:
            self.copy(c, d).wait_send()


def kernel(
    chunks, blk, wg_hbm, wu_hbm, wd_hbm, out_ref,
    er, el, odd_r, odd_l, wm, xb, xs, wg, wu, wd,
    pa, pb, ra1, rb1, qa, qb, ra2, rb2, ha, hb, ob, os_, or_,
    szl, zl, szr, zr, sol, zol, sor, zor,
    w_sem, er_s, er_r, el_s, el_r, or_s, or_r, ol_s, ol_r, x_s, x_r, o_s, o_r,
    zl_s, zl_r, zr_s, zr_r, zol_s, zol_r, zor_s, zor_r,
    a1_s, a1_r, b1_s, b1_r, a2_s, a2_r, b2_s, b2_r,
    ga1_s, ga1_r, gb1_s, gb1_r, ga2_s, ga2_r, gb2_s, gb2_r,
):
    features, block = out_ref.shape[1], out_ref.shape[0]
    part, sub = block // 2, block // SUBS
    grp, loc = lax.axis_index("grp"), lax.axis_index("loc")
    depth = lax.axis_size("loc") // 2
    x, y = grp // SIDE, lax.rem(grp, SIDE)
    z, core = loc // 2, lax.rem(loc, 2)
    x_peers = [(lax.rem(x + d, SIDE) * SIDE + y, loc) for d in range(SIDE)]
    y_peers = [(x * SIDE + lax.rem(y + d, SIDE), loc) for d in range(SIDE)]
    z_right, z_right2, z_left, z_left2 = (
        (grp, lax.rem(z + d, depth) * 2 + core) for d in (1, 2, depth - 1, depth - 2)
    )
    sibling = (grp, z * 2 + 1 - core)

    weight_copies = [
        pltpu.make_async_copy(wg_hbm.at[0], wg.at[pl.ds(META, features)], w_sem.at[0]),
        pltpu.make_async_copy(wu_hbm.at[0], wu.at[pl.ds(META, features)], w_sem.at[1]),
        pltpu.make_async_copy(wd_hbm.at[0], wd, w_sem.at[2]),
    ]
    barrier = pltpu.get_barrier_semaphore()
    neighbours = x_peers[1:] + y_peers[1:] + [z_right, z_right2, z_left, z_left2, sibling]
    for device in neighbours:
        pl.semaphore_signal(barrier, inc=1, device_id=device, device_id_type=MESH)
    el[0] = blk[...]
    wg[:META, :] = jnp.zeros((META, wg.shape[1]), BF16)
    wu[:META, :] = jnp.zeros((META, wu.shape[1]), BF16)
    for copy in weight_copies:
        copy.start()
    pl.semaphore_wait(barrier, len(neighbours))

    def half(ref, k, h):
        return ref.at[k, pl.ds(h * part, part)]

    def even_right(k, h, ref, j):
        return remote(half(ref, j, h), half(er, k, h), er_s.at[k, h], er_r.at[k, h], z_right2)

    def even_left(k, h, ref, j):
        return remote(half(ref, j, h), half(el, k, h), el_s.at[k, h], el_r.at[k, h], z_left2)

    def odd_right(k, ref, j):
        return remote(ref.at[j], odd_r.at[k], or_s.at[k], or_r.at[k], z_right)

    def odd_left(k, ref, j):
        return remote(ref.at[j], odd_l.at[k], ol_s.at[k], ol_r.at[k], z_left)

    for h in range(2):
        even_right(0, h, el, 0).start()
        even_left(1, h, el, 0).start()
    odd_right(0, el, 0).start()
    odd_left(0, el, 0).start()

    slots = wm.shape[2]
    row = lax.broadcasted_iota(jnp.int32, (slots, block), 0)
    mine = row < slots // 2
    slot = jnp.where(mine, row, row - slots // 2).astype(F32)
    earlier = (
        lax.broadcasted_iota(jnp.int32, (block, block), 0)
        < lax.broadcasted_iota(jnp.int32, (block, block), 1)
    ).astype(F32).astype(BF16)
    expert = loc.astype(F32)
    other = (z * 2 + 1 - core).astype(F32)

    def place(ref, k):
        meta = ref[k, :16, :META].astype(F32)
        ids, weights = meta[:8], meta[8:]
        hit, hit_other = ids == expert, ids == other
        count = lambda v: jnp.sum(v, axis=0, keepdims=True)
        hits = jnp.where(
            mine, count(jnp.where(hit, 1.0, 0.0)), count(jnp.where(hit_other, 1.0, 0.0))
        )
        scale = jnp.where(
            mine, count(jnp.where(hit, weights, 0.0)), count(jnp.where(hit_other, weights, 0.0))
        )
        position = jnp.dot(hits.astype(BF16), earlier, preferred_element_type=F32)
        chosen = jnp.where(position == slot, hits, 0.0)
        rows = jnp.dot(chosen.astype(BF16), ref[k], preferred_element_type=F32).astype(BF16)
        return rows, (chosen * scale).astype(BF16)

    def x_copy(c):
        return remote(xs.at[c], xb.at[c, 1], x_s.at[c], x_r.at[c], sibling)

    def o_copy(c):
        return remote(os_.at[c], or_.at[c], o_s.at[c], o_r.at[c], sibling)

    def gather_step(k):
        for h in range(2):
            even_right(k, h, el, 0).wait_recv()

            @pl.when(k < chunks - 1)
            def _():
                even_right(k + 1, h, er, k).start()

            @pl.when(k > 0)
            def _():
                even_left(k, h, el, 0).wait_recv()

            @pl.when(jnp.logical_and(k > 0, k < chunks - 1))
            def _():
                even_left(k + 1, h, el, k).start()

        @pl.when(k < chunks - 1)
        def _():
            odd_right(k + 1, er, k).start()

        @pl.when(k > 0)
        def _():
            odd_left(k, el, k).start()

    def place_all(k):
        odd_right(k, el, 0).wait_recv()
        odd_left(k, el, 0).wait_recv()
        got = [place(ref, k) for ref in (er, el, odd_r, odd_l)]
        for i, (rows, weights) in enumerate(got):
            wm[k, i] = weights
            xb[k, 0, i * 16:(i + 1) * 16, :] = rows[:16]
            xs[k, i * 16:(i + 1) * 16, :] = rows[16:]
        x_copy(k).start()

    sum_a1 = Scatter(pa, x, x_peers, ra1, a1_s, a1_r)
    sum_b1 = Scatter(pb, y, y_peers, rb1, b1_s, b1_r)
    sum_a2 = Scatter(qa, y, y_peers, ra2, a2_s, a2_r)
    sum_b2 = Scatter(qb, x, x_peers, rb2, b2_s, b2_r)
    gather_a1 = Gather(lambda c, i: ha.at[c, x, i], y, y_peers, ga1_s, ga1_r)
    gather_b1 = Gather(lambda c, i: hb.at[c, y, i], x, x_peers, gb1_s, gb1_r)
    gather_a2 = Gather(lambda c, i: ha.at[c, i], x, x_peers, ga2_s, ga2_r)
    gather_b2 = Gather(lambda c, i: hb.at[c, i], y, y_peers, gb2_s, gb2_r)
    piece = pa.shape[4]

    def expand(c):
        x_copy(c).wait_recv()
        held = jnp.concatenate([xb[c, 0], xb[c, 1]], axis=0)
        for n in range(SIDE):
            for k, weight in enumerate((wg, wu)):
                term = jnp.dot(
                    held, weight[:, n * 256:(n + 1) * 256], preferred_element_type=F32
                ).astype(BF16)
                for i in range(SIDE):
                    low, lane = (i % 2) * piece, (i // 2) * 128
                    pa[c, n, k, i] = term[low:low + piece, lane:lane + 128]
                    pb[c, i, k, n] = term[2 * piece + low:3 * piece + low, lane:lane + 128]
        sum_a1.start(c)
        sum_b1.start(c)

    def stage2(c):
        for ring, to, then in ((sum_a1, qa, sum_a2), (sum_b1, qb, sum_b2)):
            total = ring.total(c).astype(BF16)
            for i in range(SIDE):
                to[c, i] = total[:, i]
            then.start(c)

    def stage3(c):
        total = sum_a2.total(c)
        ha[c, x, y] = (total[0] / (1.0 + jnp.exp(-total[0])) * total[1]).astype(BF16)
        gather_a1.start(c)
        total = sum_b2.total(c)
        hb[c, y, x] = (total[0] / (1.0 + jnp.exp(-total[0])) * total[1]).astype(BF16)
        gather_b1.start(c)

    def stage4(c):
        gather_a1.wait(c)
        gather_a2.start(c)
        gather_b1.wait(c)
        gather_b2.start(c)

    def contract(c):
        gather_a2.wait(c)
        gather_b2.wait(c)
        lines = [
            jnp.concatenate([ha[c, u, 2 * v + low] for u in range(SIDE) for v in range(2)], axis=1)
            for low in range(2)
        ] + [
            jnp.concatenate([hb[c, 2 * v + low, u] for u in range(SIDE) for v in range(2)], axis=1)
            for low in range(2)
        ]
        result = lax.dot_general(
            jnp.concatenate(lines, axis=0), wd[...], (((1,), (1,)), ((), ())),
            preferred_element_type=F32,
        ).astype(BF16)
        for i in range(4):
            ob[c, i, :, :features] = result[i * 16:(i + 1) * 16]
            os_[c, i, :, :features] = result[64 + i * 16:64 + (i + 1) * 16]
        o_copy(c).start()

    def to_left2(k, h):
        return remote(szl.at[k, h], zl.at[k, h], zl_s.at[k, h], zl_r.at[k, h], z_left2)

    def to_right2(k, h):
        return remote(szr.at[k, h], zr.at[k, h], zr_s.at[k, h], zr_r.at[k, h], z_right2)

    def to_left(k):
        return remote(sol.at[k], zol.at[k], zol_s.at[k], zol_r.at[k], z_left)

    def to_right(k):
        return remote(sor.at[k], zor.at[k], zor_s.at[k], zor_r.at[k], z_right)

    def share(k, i):
        held = jnp.concatenate([ob[k, i, :, :features], or_[k, i, :, :features]], axis=0)
        return lax.dot_general(
            wm[k, i], held, (((0,), (0,)), ((), ())), preferred_element_type=F32
        )

    def odd_shares(c):
        o_copy(c).wait_recv()
        sol[c, :, :features] = share(c, 2).astype(BF16)
        to_left(c).start()
        sor[c, :, :features] = share(c, 3).astype(BF16)
        to_right(c).start()

    def when(lag, t, stage):
        c = t - lag

        @pl.when(jnp.logical_and(c >= 0, c < chunks))
        def _():
            stage(c)

    def turn(t, carry):
        when(0, t, gather_step)

        @pl.when(t == 0)
        def _():
            for copy in weight_copies:
                copy.wait()

        when(1, t, place_all)
        when(2, t, stage2)
        when(1, t, expand)
        when(3, t, stage3)
        when(4, t, stage4)
        when(6, t, odd_shares)
        when(5, t, contract)
        return carry

    lax.fori_loop(0, chunks + 6, turn, 0)

    def back(k, first=False, last=False):
        left_share = share(k, 0)
        if not first:
            to_left(k + 1).wait_recv()
        if not last:
            right_share = share(k, 1)
            to_right(k).wait_recv()
        for h in range(SUBS):
            rows = slice(h * sub, (h + 1) * sub)
            total = left_share[rows]
            if not first:
                total = total + zol[k + 1, rows, :features].astype(F32)
                to_left2(k + 1, h).wait_recv()
                total = total + zl[k + 1, h, :, :features].astype(F32)
            szl[k, h, :, :features] = total.astype(BF16)
            to_left2(k, h).start()
            if not last:
                total = right_share[rows] + zor[k, rows, :features].astype(F32)
                if not first:
                    to_right2(k + 1, h).wait_recv()
                    total = total + zr[k + 1, h, :, :features].astype(F32)
                szr[k, h, :, :features] = total.astype(BF16)
                to_right2(k, h).start()

    def back_turn(i, carry):
        back(chunks - 2 - i)
        return carry

    back(chunks - 1, first=True)
    lax.fori_loop(0, chunks - 2, back_turn, 0)
    back(0, last=True)
    own = share(0, 1)
    to_left(0).wait_recv()
    to_right(0).wait_recv()
    for h in range(SUBS):
        rows = slice(h * sub, (h + 1) * sub)
        to_left2(0, h).wait_recv()
        to_right2(1, h).wait_recv()
        out_ref[rows, :] = (
            own[rows]
            + zol[0, rows, :features].astype(F32)
            + zor[0, rows, :features].astype(F32)
            + zl[0, h, :, :features].astype(F32)
            + zr[1, h, :, :features].astype(F32)
        ).astype(BF16)

    def finish(k, carry):
        x_copy(k).wait_send()
        o_copy(k).wait_send()
        for stage in (
            sum_a1, sum_b1, sum_a2, sum_b2, gather_a1, gather_b1, gather_a2, gather_b2,
        ):
            stage.finish(k)
        odd_right(k, el, 0).wait_send()
        odd_left(k, el, 0).wait_send()
        to_left(k).wait_send()
        to_right(k).wait_send()
        for h in range(2):
            even_right(k, h, el, 0).wait_send()
        for h in range(SUBS):
            to_left2(k, h).wait_send()

        @pl.when(k > 0)
        def _():
            for h in range(2):
                even_left(k, h, el, 0).wait_send()
            for h in range(SUBS):
                to_right2(k, h).wait_send()

        return carry

    lax.fori_loop(0, chunks, finish, 0)


def shards(tokens, expert_ids, route_weight, w_gate, w_up, w_down):
    block, features = tokens.shape
    top = expert_ids.shape[1]
    chunks = lax.axis_size("loc") // 8
    units = w_gate.shape[2]
    wide = features + META
    meta = jnp.concatenate([expert_ids.astype(BF16).T, route_weight.astype(BF16).T], axis=0)
    meta = jnp.pad(meta, ((0, block - 2 * top), (0, META - block)))
    blk = jnp.concatenate([meta, tokens], axis=1)
    piece = 32
    sem = lambda *shape: pltpu.SemaphoreType.DMA(shape)
    vmem = lambda *shape: pltpu.VMEM(shape, BF16)
    ring = (SIDE, piece, 128)
    blocks = (chunks, block, wide)
    subs = (chunks, SUBS, block // SUBS, wide)
    scratch = (
        [vmem(*blocks)] * 4
        + [vmem(chunks, 4, 32, block), vmem(chunks, 2, 64, wide), vmem(chunks, 64, wide)]
        + [vmem(wide, units), vmem(wide, units), vmem(features, units)]
        + [vmem(chunks, SIDE, 2, *ring)] * 2
        + [vmem(chunks, 3, 2, *ring)] * 2
        + [vmem(chunks, SIDE, 2, piece, 128)] * 2
        + [vmem(chunks, 3, 2, piece, 128)] * 2
        + [vmem(chunks, SIDE, *ring)] * 2
        + [vmem(chunks, 4, 16, wide)] * 3
        + [vmem(*subs)] * 4
        + [vmem(*blocks)] * 4
        + [sem(3)]
        + [sem(chunks, 2)] * 4
        + [sem(chunks)] * 8
        + [sem(chunks, SUBS)] * 4
        + [sem(chunks)] * 4
        + [sem(chunks, 3)] * 16
    )
    rows = chunks * 128
    return pl.pallas_call(
        functools.partial(kernel, chunks),
        out_shape=jax.ShapeDtypeStruct((block, features), BF16),
        in_specs=[pl.BlockSpec(memory_space=pltpu.VMEM)]
        + [pl.BlockSpec(memory_space=pl.ANY)] * 3,
        out_specs=pl.BlockSpec(memory_space=pltpu.VMEM),
        scratch_shapes=scratch,
        compiler_params=pltpu.CompilerParams(
            collective_id=0, has_side_effects=True, vmem_limit_bytes=48 * 1024 * 1024
        ),
        cost_estimate=pl.CostEstimate(
            flops=6 * rows * features * units,
            bytes_accessed=6 * features * units,
            transcendentals=0,
        ),
    )(blk, w_gate, w_up, jnp.swapaxes(w_down, 1, 2))


def solution(mesh):
    in_specs = (
        P("loc", "grp"),
        P("loc", None),
        P("loc", None),
        P("loc", "grp", None),
        P("loc", "grp", None),
        P("loc", None, "grp"),
    )
    out_specs = P("loc", "grp")
    return jax.shard_map(shards, mesh=mesh, in_specs=in_specs, out_specs=out_specs, check_vma=False)
```

time: 491 us -> 145 us (0.30)
  waiting for transfers between devices: 289 us -> 0 us
  blocking collectives: 140 us -> 0 us
  Pallas kernels: 0 us -> 139 us
  starting transfers between devices: 23.6 us -> 0 us
  between operations: 13.5 us -> 0.03 us
  matrix products: 8.09 us -> 0 us
  local copies, waits for them, and re-layouts: 9.95 us -> 4.17 us
  other arithmetic: 6.89 us -> 1.64 us
    all_to_all x1 -> x0, blocking collectives: 140 us -> none  [shards(): lax.all_to_all(outgoing, 'loc', split_axis=0, concat_axis=0, tiled=True)]
    pallas_call x0 -> x1, Pallas kernels: none -> 139 us  [shards(): pl.pallas_call(functools.partial(kernel, chunks), out_shape=jax.ShapeDtyp...]
    all_to_all x1 -> x0, waiting for transfers between devices: 111 us -> none  [shards(): lax.all_to_all(expert_out, 'loc', split_axis=0, concat_axis=0, tiled=True)]
    reduce_scatter x1 -> x0, waiting for transfers between devices: 94.5 us -> none  [shards(): lax.psum_scatter(jnp.concatenate([gate_term, up_term], axis=1).astype(jnp...]
    all_gather x1 -> x0, waiting for transfers between devices: 83.4 us -> none  [shards(): lax.all_gather(hidden, 'grp', axis=0, tiled=True)]
    all_to_all x1 -> x0, starting transfers between devices: 23.5 us -> none  [shards(): lax.all_to_all(expert_out, 'loc', split_axis=0, concat_axis=0, tiled=True)]
    dot_general x5 -> x0, matrix products: 8.09 us -> none  [the longest x1 2.72 us: shards(): lax.dot_general(lax.all_gather(hidden, 'grp', axis=0, tiled=True), down_p...]
  transfers between devices with their start and end apart: 3 -> 0, of which waited for: 3 -> 0; matrix products, arithmetic and copies ran while one was open for 0% -> 0% of each run, Pallas kernels for 0% -> 0%
where the time goes in v2:
time: 145 us
  Pallas kernels  139 us (96%)
  local copies, waits for them, and re-layouts  4.17 us (3%)
  other arithmetic  1.64 us (1%)
    pallas_call x1, Pallas kernels, shards(): pl.pallas_call(functools.partial(kernel, chunks), out_shape=jax.ShapeDtyp...  139 us
    unnamed x9, local copies, waits for them, and re-layouts  4.17 us

profile of v2, /device:TPU:2, one launch (start us, length us, event | category | flops | bytes accessed | tf_op | source)
XLA Modules:
  0.0 144.7 jit_solution(9212759558994648704)
XLA Ops:
  0.0 0.0 copy-start.3
  0.0 0.7 convert_bitcast_fusion.1
  0.7 0.0 copy-done.3
  0.7 0.9 pad_maximum_fusion.blk
  1.7 0.0 copy-start
  1.7 1.2 copy-done
  2.8 0.0 copy-start.1
  2.8 1.2 copy-done.1
  4.0 0.0 copy-start.2
  4.0 1.2 copy-done.2
  5.2 138.9 %shard_map.64 = bf16[64,448]{1,0:T(8,128)(2,1)S(1)} custom-call(bf16[64,512]{1,0:T(8,128)(2,1)S(1)} %pad_maximum_fusion.blk, bf16[1,448,1024]{2,1,0:T(8,128)(2,1)S(1)} %copy-done, bf16[1,448,1024]{2,1,0:T(8,128)(2,1)S(1)} %copy-done.1, bf16[1,448,1024]{2,1,0:T(8,128)(2,1)S(1)} %bitcast.5), custom_call_target="tpu_custom_call" | custom-call | flops 2818572288 | bytes 2752512 | tf_op jit(solution)/shard_map/pallas_call | solution.py:434
  144.1 0.6 copy.8
  (2 shorter events, 0.0 us)
Async XLA Ops:
  0.0 0.7 copy-start.3
  1.7 1.2 copy-start
  2.8 1.2 copy-start.1
  4.0 1.2 copy-start.2

commit v3 on v2

--- a/solution.py
+++ b/solution.py
@@ -80,7 +80,7 @@
 
 
 def kernel(
-    chunks, blk, wg_hbm, wu_hbm, wd_hbm, out_ref,
+    chunks, tokens, ids_t, weights_t, wg_hbm, wu_hbm, wd_hbm, out_ref,
     er, el, odd_r, odd_l, wm, xb, xs, wg, wu, wd,
     pa, pb, ra1, rb1, qa, qb, ra2, rb2, ha, hb, ob, os_, or_,
     szl, zl, szr, zr, sol, zol, sor, zor,
@@ -111,7 +111,11 @@
     neighbours = x_peers[1:] + y_peers[1:] + [z_right, z_right2, z_left, z_left2, sibling]
     for device in neighbours:
         pl.semaphore_signal(barrier, inc=1, device_id=device, device_id_type=MESH)
-    el[0] = blk[...]
+    el[0, :, META:] = tokens[...]
+    el[0, 16:, :META] = jnp.zeros((block - 16, META), BF16)
+    el[0, :16, :META] = jnp.concatenate(
+        [ids_t[...].astype(F32), weights_t[...]], axis=0
+    ).astype(BF16)
     wg[:META, :] = jnp.zeros((META, wg.shape[1]), BF16)
     wu[:META, :] = jnp.zeros((META, wu.shape[1]), BF16)
     for copy in weight_copies:
@@ -398,13 +402,9 @@
 
 def shards(tokens, expert_ids, route_weight, w_gate, w_up, w_down):
     block, features = tokens.shape
-    top = expert_ids.shape[1]
     chunks = lax.axis_size("loc") // 8
     units = w_gate.shape[2]
     wide = features + META
-    meta = jnp.concatenate([expert_ids.astype(BF16).T, route_weight.astype(BF16).T], axis=0)
-    meta = jnp.pad(meta, ((0, block - 2 * top), (0, META - block)))
-    blk = jnp.concatenate([meta, tokens], axis=1)
     piece = 32
     sem = lambda *shape: pltpu.SemaphoreType.DMA(shape)
     vmem = lambda *shape: pltpu.VMEM(shape, BF16)
@@ -434,19 +434,19 @@
     return pl.pallas_call(
         functools.partial(kernel, chunks),
         out_shape=jax.ShapeDtypeStruct((block, features), BF16),
-        in_specs=[pl.BlockSpec(memory_space=pltpu.VMEM)]
-        + [pl.BlockSpec(memory_space=pl.ANY)] * 3,
+        in_specs=[pl.BlockSpec(memory_space=pltpu.VMEM)] * 3
+        + [pl.BlockSpec(memory_space=pltpu.HBM)] * 3,
         out_specs=pl.BlockSpec(memory_space=pltpu.VMEM),
         scratch_shapes=scratch,
         compiler_params=pltpu.CompilerParams(
-            collective_id=0, has_side_effects=True, vmem_limit_bytes=48 * 1024 * 1024
+            collective_id=0, has_side_effects=True, vmem_limit_bytes=60 * 1024 * 1024
         ),
         cost_estimate=pl.CostEstimate(
             flops=6 * rows * features * units,
             bytes_accessed=6 * features * units,
             transcendentals=0,
         ),
-    )(blk, w_gate, w_up, jnp.swapaxes(w_down, 1, 2))
+    )(tokens, expert_ids.T, route_weight.T, w_gate, w_up, jnp.swapaxes(w_down, 1, 2))
 
 
 def solution(mesh):

time: 145 us -> 142 us (0.979)
  the two profiles are of different devices: /device:TPU:2 before, /device:TPU:64 now
where the time goes in v3:
time: 142 us
  Pallas kernels  141 us (99%)
  local copies, waits for them, and re-layouts  1.47 us (1%)
    pallas_call x1, Pallas kernels, shards(): pl.pallas_call(functools.partial(kernel, chunks), out_shape=jax.ShapeDtyp...  141 us

profile of v3, /device:TPU:64, one launch (start us, length us, event | category | flops | bytes accessed | tf_op | source)
XLA Modules:
  0.0 142.1 jit_solution(532664099427833649)
XLA Ops:
  0.0 140.7 %shard_map.64 = bf16[64,448]{1,0:T(8,128)(2,1)} custom-call(bf16[64,448]{1,0:T(8,128)(2,1)} %tokens.1, s32[8,64]{1,0:T(8,128)} %bitcast.4, f32[8,64]{1,0:T(8,128)} %bitcast.5, bf16[1,448,1024]{2,1,0:T(8,128)(2,1)} %wg_hbm.1, bf16[1,448,1024]{2,1,0:T(8,128)(2,1)} %wu_hbm.1, bf16[1,448,1024]{2,1,0:T(8,128)(2,1)} %bitcast.3), custom_call_target="tpu_custom_call" | custom-call | flops 2818572288 | bytes 2752512 | tf_op jit(solution)/shard_map/pallas_call | solution.py:434
  140.7 1.5 %copy.8 = bf16[64,448]{1,0:T(8,128)(2,1)} copy(bf16[64,448]{1,0:T(8,128)(2,1)} %shard_map.64) | data formatting | bytes 114688
